TPU v7x, 32 devices: a whole 2x2x4 slice. The times are simulated.
32 devices in a mesh: member: 4 (over y, x), fsdp: 8 (over z, core).
Axes of the slice: x: 2, y: 2, z: 4, core: 2. Of those that a mesh axis runs over, the one named last changes fastest.
Arguments:
- tokens: bfloat16 [4, 1024, 2048], P('member', 'fsdp'), may hold values from -6 to 6
- out_grad: bfloat16 [4, 1024, 8192], P('member', 'fsdp'), may hold values from -2 to 2
- master: float32 [4, 2048, 8192], P('member', None, 'fsdp'), may hold values from -0.125 to 0.125
- first_moment: bfloat16 [4, 2048, 8192], P('member', None, 'fsdp'), may hold values from -6 to 6
- second_moment: bfloat16 [4, 2048, 8192], P('member', None, 'fsdp'), may hold values from 1 to 100
- source: int32 [4], replicated, may hold values from 0 to 3, as said below
- perturb: int32 [4], replicated, may hold values from 0 to 3
Outputs:
- new_master: float32 [4, 2048, 8192], P('member', None, 'fsdp')
- new_first: bfloat16 [4, 2048, 8192], P('member', None, 'fsdp')
- new_second: bfloat16 [4, 2048, 8192], P('member', None, 'fsdp')
- gate_out: bfloat16 [4, 1024, 8192], P('member', None, 'fsdp')
Inputs may be any that keep to these rules, and one draw needn't show every extreme that they name: Exactly 1 members i have source[i] != i; every member named as a source has its own index as source.
All inputs are finite; a program needn't handle non-finite values.
Results may differ from a plain program's by a relative error of at most 0.0049.
Values may be sent and summed in bfloat16 or wider, within the bound.
A program may use at most 128 MiB of HBM per device.

v0:
```python
import functools
import jax
import numpy as np
import jax.numpy as jnp
from jax import lax
from jax.experimental import pallas as pl
from jax.experimental.pallas import tpu as pltpu
from jax.sharding import PartitionSpec as P

rate_factors = (0.5, 0.8, 1.25, 2.0)
base_rate = 0.02
decay = 0.1
epsilon = 1e-08
MESH = pl.DeviceIdType.MESH
MIB = 1024 * 1024


def routes(loser, anchor):
    apart = loser ^ anchor
    if apart == 3:
        return [(anchor, anchor ^ 1, loser), (anchor, anchor ^ 2, loser)]
    other = 3 - apart
    return [(anchor, loser), (anchor, anchor ^ other, loser ^ other, loser)]


def exchange_kernel(
    loser, anchor, chunk,
    tokens, out_grad, master, first, second,
    gathered, cols, got_master, got_first, got_second,
    wide, narrow, token_send, token_recv, grad_send, grad_recv,
    state_send, state_recv, local_sem,
):
    members = lax.axis_size("member")
    ring = lax.axis_size("fsdp")
    mine = lax.axis_index("fsdp")
    member = lax.axis_index("member")
    rows = tokens.shape[1]
    width = cols.shape[1]

    barrier = pltpu.get_barrier_semaphore()
    for step in range(1, ring):
        pl.semaphore_signal(
            barrier, inc=1, device_id={"fsdp": lax.rem(mine + step, ring)}, device_id_type=MESH
        )
    for step in range(1, members):
        pl.semaphore_signal(
            barrier, inc=1, device_id={"member": lax.rem(member + step, members)}, device_id_type=MESH
        )
    pl.semaphore_wait(barrier, ring + members - 2)

    ways = routes(loser, anchor)
    depth = master.shape[1]
    pieces = depth // chunk
    split = pieces // 2 if len(ways[0]) == len(ways[1]) else pieces // 2 + 1
    spans = ((0, split), (split, pieces))
    landing = (got_first, got_second, got_master)
    starting = (first.at[0], second.at[0], narrow)

    def state_copy(kind, piece, origin, target):
        at = pl.ds(pl.multiple_of(piece * chunk, chunk), chunk)
        return pltpu.make_async_remote_copy(
            src_ref=(starting if origin else landing)[kind].at[at],
            dst_ref=landing[kind].at[at],
            send_sem=state_send.at[kind, piece],
            recv_sem=state_recv.at[kind, piece],
            device_id={"member": target},
            device_id_type=MESH,
        )

    load = pltpu.make_async_copy(master.at[0], wide, local_sem.at[0])

    @pl.when(member == anchor)
    def _():
        load.start()
        for kind in (0, 1):
            for way, (low, high) in reversed(tuple(zip(ways, spans))):
                @pl.loop(low, high)
                def _(piece):
                    state_copy(kind, piece, True, way[1]).start()

    my_rows = pl.ds(pl.multiple_of(mine * rows, rows), rows)

    def token_copy(step):
        return pltpu.make_async_remote_copy(
            src_ref=tokens.at[0],
            dst_ref=gathered.at[my_rows],
            send_sem=token_send.at[step],
            recv_sem=token_recv.at[step],
            device_id={"fsdp": lax.rem(mine + step, ring)},
            device_id_type=MESH,
        )

    def grad_copy(step):
        target = lax.rem(mine + step, ring)
        return pltpu.make_async_remote_copy(
            src_ref=out_grad.at[0, :, pl.ds(pl.multiple_of(target * width, width), width)],
            dst_ref=cols.at[my_rows],
            send_sem=grad_send.at[step],
            recv_sem=grad_recv.at[step],
            device_id={"fsdp": target},
            device_id_type=MESH,
        )

    for step in range(1, ring):
        grad_copy(step).start()
        token_copy(step).start()
    own_tokens = pltpu.make_async_copy(tokens.at[0], gathered.at[my_rows], local_sem.at[1])
    own_grad = pltpu.make_async_copy(
        out_grad.at[0, :, pl.ds(pl.multiple_of(mine * width, width), width)],
        cols.at[my_rows],
        local_sem.at[2],
    )
    own_tokens.start()
    own_grad.start()

    @pl.when(member == anchor)
    def _():
        load.wait()
        for way, (low, high) in reversed(tuple(zip(ways, spans))):
            @pl.loop(low, high)
            def _(piece):
                at = pl.ds(pl.multiple_of(piece * chunk, chunk), chunk)
                narrow[at, :] = wide[at, :].astype(narrow.dtype)
                state_copy(2, piece, True, way[1]).start()

    for way, (low, high) in zip(ways, spans):
        for here in range(1, len(way) - 1):
            @pl.when(member == way[here])
            def _():
                for kind in range(3):
                    @pl.loop(low, high)
                    def _(piece):
                        passed = state_copy(kind, piece, False, way[here + 1])
                        passed.wait_recv()
                        passed.start()

    for step in range(1, ring):
        grad_copy(step).wait()
        token_copy(step).wait()
    own_tokens.wait()
    own_grad.wait()

    for way, (low, high) in zip(ways, spans):
        @pl.when(member == way[-1])
        def _():
            for kind in range(3):
                @pl.loop(low, high)
                def _(piece):
                    state_copy(kind, piece, False, way[-2]).wait_recv()

        for here in range(len(way) - 1):
            @pl.when(member == way[here])
            def _():
                for kind in range(3):
                    @pl.loop(low, high)
                    def _(piece):
                        state_copy(kind, piece, here == 0, way[here + 1]).wait_send()


def exchange(loser, anchor, number, tokens, out_grad, master, first, second):
    ring = lax.axis_size("fsdp")
    _, rows, depth = tokens.shape
    width = master.shape[2]
    chunk = 32
    pieces = depth // chunk
    half = jax.ShapeDtypeStruct((depth, width), jnp.bfloat16)
    spot = pl.BlockSpec(memory_space=pl.ANY)
    return pl.pallas_call(
        functools.partial(exchange_kernel, loser, anchor, chunk),
        out_shape=(
            jax.ShapeDtypeStruct((ring * rows, depth), tokens.dtype),
            jax.ShapeDtypeStruct((ring * rows, width), out_grad.dtype),
            half,
            half,
            half,
        ),
        in_specs=[spot] * 5,
        out_specs=[spot] * 5,
        scratch_shapes=[
            pltpu.VMEM((depth, width), jnp.float32),
            pltpu.VMEM((depth, width), jnp.bfloat16),
            pltpu.SemaphoreType.DMA((ring,)),
            pltpu.SemaphoreType.DMA((ring,)),
            pltpu.SemaphoreType.DMA((ring,)),
            pltpu.SemaphoreType.DMA((ring,)),
            pltpu.SemaphoreType.DMA((3, pieces)),
            pltpu.SemaphoreType.DMA((3, pieces)),
            pltpu.SemaphoreType.DMA((3,)),
        ],
        compiler_params=pltpu.CompilerParams(
            collective_id=number, has_side_effects=True, vmem_limit_bytes=40 * MIB
        ),
    )(tokens, out_grad, master, first, second)


def update_kernel(
    source, perturb, place, inputs, cols, own_master, own_first, own_second, got_master, got_first, got_second,
    new_master, new_first, new_second, gate_out, total,
):
    step = pl.program_id(0)
    is_taken = source[place[0]] != place[0]
    level = perturb[place[0]]
    rate = jnp.float32(0.0)
    for index, factor in enumerate(rate_factors):
        rate = jnp.where(level == index, np.float32(base_rate) * np.float32(factor), rate)
    block = inputs[...]
    grad = lax.dot_general(
        block, cols[...], (((0,), (0,)), ((), ())), preferred_element_type=jnp.float32
    )
    weight = jnp.where(is_taken, got_master[...].astype(jnp.float32), own_master[0])
    first_old = jnp.where(is_taken, got_first[...], own_first[0]).astype(jnp.float32)
    second_old = jnp.where(is_taken, got_second[...], own_second[0]).astype(jnp.float32)
    first = 0.9 * first_old + 0.1 * grad
    second = 0.95 * second_old + 0.05 * grad * grad
    updated = weight - rate * (first / (jnp.sqrt(second) + epsilon) + decay * weight)
    new_master[0] = updated
    new_first[0] = first.astype(jnp.bfloat16)
    new_second[0] = second.astype(jnp.bfloat16)
    part = jnp.dot(block, updated.astype(jnp.bfloat16), preferred_element_type=jnp.float32)

    @pl.when(step == 0)
    def _():
        total[...] = part

    @pl.when(step > 0)
    def _():
        total[...] += part

    @pl.when(step == pl.num_programs(0) - 1)
    def _():
        gate_out[0] = total[...].astype(jnp.bfloat16)


def update(source, perturb, place, gathered, cols, master, first, second, got_master, got_first, got_second):
    count, depth = gathered.shape
    width = cols.shape[1]
    block = 256

    own = pl.BlockSpec(
        (1, block, width), lambda i, s, p, m: (0, jnp.where(s[m[0]] == m[0], i, 0), 0)
    )
    got = pl.BlockSpec((block, width), lambda i, s, p, m: (jnp.where(s[m[0]] == m[0], 0, i), 0))
    new = pl.BlockSpec((1, block, width), lambda i, s, p, m: (0, i, 0))
    return pl.pallas_call(
        update_kernel,
        out_shape=(
            jax.ShapeDtypeStruct((1, depth, width), jnp.float32),
            jax.ShapeDtypeStruct((1, depth, width), jnp.bfloat16),
            jax.ShapeDtypeStruct((1, depth, width), jnp.bfloat16),
            jax.ShapeDtypeStruct((1, count, width), jnp.bfloat16),
        ),
        grid_spec=pltpu.PrefetchScalarGridSpec(
            num_scalar_prefetch=3,
            grid=(depth // block,),
            in_specs=[
                pl.BlockSpec((count, block), lambda i, s, p, m: (0, i)),
                pl.BlockSpec((count, width), lambda i, s, p, m: (0, 0)),
                own, own, own, got, got, got,
            ],
            out_specs=[
                new, new, new,
                pl.BlockSpec((1, count, width), lambda i, s, p, m: (0, 0, 0)),
            ],
            scratch_shapes=[pltpu.VMEM((count, width), jnp.float32)],
        ),
        compiler_params=pltpu.CompilerParams(vmem_limit_bytes=52 * MIB),
    )(source, perturb, place, gathered, cols, master, first, second, got_master, got_first, got_second)


def rate_of(perturb, member_index, positions):
    my_level = jnp.sum(jnp.where(positions == member_index, perturb, 0))
    table = jnp.array(rate_factors, dtype=jnp.float32)
    levels = jnp.arange(len(rate_factors), dtype=jnp.int32)
    return base_rate * jnp.sum(jnp.where(levels == my_level, table, 0.0))


def square_shards(tokens, out_grad, master, first_moment, second_moment, source, perturb):
    count = lax.axis_size("member")
    member_index = lax.axis_index("member")
    positions = jnp.arange(count, dtype=jnp.int32)
    pairs = [(i, j) for i in range(count) for j in range(count) if i != j]
    order = positions * (count - 1) + source - (source > positions).astype(jnp.int32)
    branch = jnp.sum(jnp.where(source != positions, order, 0))
    got = lax.switch(
        branch,
        [functools.partial(exchange, i, j, k) for k, (i, j) in enumerate(pairs)],
        tokens, out_grad, master, first_moment, second_moment,
    )
    gathered, cols, got_master, got_first, got_second = got
    return update(
        source, perturb, member_index[None], gathered, cols, master, first_moment, second_moment,
        got_master, got_first, got_second,
    )


def from_root(value, axis, source):
    kept = jnp.where(lax.axis_index(axis) == source, value, 0).astype(value.dtype)
    return lax.psum(kept, axis)


def general_shards(tokens, out_grad, master, first_moment, second_moment, source, perturb):
    count = lax.axis_size("member")
    member_index = lax.axis_index("member")
    positions = jnp.arange(count, dtype=jnp.int32)
    moments = jnp.stack([first_moment, second_moment], 1)
    losers_total = 3 * count // 8
    copying = source != positions
    earlier = positions[None, :] < positions[:, None]
    rank = jnp.sum(jnp.where(earlier & copying[None, :], 1, 0), axis=1)
    master_now = master
    moments_now = moments
    for turn in range(losers_total):
        target = jnp.sum(jnp.where(copying & (rank == turn), positions, 0))
        anchor = jnp.sum(jnp.where(positions == target, source, 0))
        got_master = from_root(master, "member", anchor)
        got_moments = from_root(moments, "member", anchor)
        taken = member_index == target
        master_now = jnp.where(taken, got_master, master_now)
        moments_now = jnp.where(taken, got_moments, moments_now)
    gathered = lax.all_gather(tokens, "fsdp", axis=1, tiled=True)
    grad_cols = lax.all_to_all(out_grad, "fsdp", split_axis=2, concat_axis=1, tiled=True)
    inputs = gathered[0]
    grad = lax.dot_general(
        inputs, grad_cols[0], (((0,), (0,)), ((), ())), preferred_element_type=jnp.float32
    )
    first = 0.9 * moments_now[0, 0].astype(jnp.float32) + 0.1 * grad
    second = 0.95 * moments_now[0, 1].astype(jnp.float32) + 0.05 * grad * grad
    rate = rate_of(perturb, member_index, positions)
    weight = master_now[0]
    updated = weight - rate * (first / (jnp.sqrt(second) + epsilon) + decay * weight)
    weight_half = updated.astype(jnp.bfloat16)
    gate_out = jnp.dot(inputs, weight_half, preferred_element_type=jnp.float32).astype(jnp.bfloat16)
    return (
        updated[None],
        first.astype(jnp.bfloat16)[None],
        second.astype(jnp.bfloat16)[None],
        gate_out[None],
    )


def solution(mesh):
    in_specs = (
        P("member", "fsdp", None),
        P("member", "fsdp", None),
        P("member", None, "fsdp"),
        P("member", None, "fsdp"),
        P("member", None, "fsdp"),
        P(),
        P(),
    )
    out_specs = (
        P("member", None, "fsdp"),
        P("member", None, "fsdp"),
        P("member", None, "fsdp"),
        P("member", None, "fsdp"),
    )
    shards = square_shards if mesh.shape["member"] == 4 else general_shards
    return jax.shard_map(shards, mesh=mesh, in_specs=in_specs, out_specs=out_specs, check_vma=False)
```

profile of v0, /device:TPU:2, one launch (start us, length us, event | category | flops | bytes accessed | tf_op | source)
XLA Modules:
  0.0 175.1 jit_solution(9204446329075333481)
XLA Ops:
  0.6 1.3 fusion
  2.6 0.0 copy-start
  2.6 0.0 copy-start.1
  2.6 148.4 %conditional.1 = ((bf16[1024,2048]{1,0:T(8,128)(2,1)}, bf16[1024,1024]{1,0:T(8,128)(2,1)S(1)}, bf16[2048,1024]{1,0:T(8,128)(2,1)}, bf16[2048,1024]{1,0:T(8,128)(2,1)}, bf16[2048,1024]{1,0:T(8,128)(2,1)})) conditional(s32[]{:T(128)} %clamp.3, (bf16[1,128,2048]{2,1,0:T(8,128)(2,1)}, bf16[1,128,8192]{2,1,0:T(8,128)(2,1)}, ...), branch_computations={%region_1.2_spmd, %region_2.3_spmd, %region_3.4_spmd, %region_4.5_... | conditional | bytes 8 | solution.py:284
  2.8 148.0 %branch_10_fun.1 = (bf16[1024,2048]{1,0:T(8,128)(2,1)}, bf16[1024,1024]{1,0:T(8,128)(2,1)S(1)}, bf16[2048,1024]{1,0:T(8,128)(2,1)}, bf16[2048,1024]{1,0:T(8,128)(2,1)}, bf16[2048,1024]{1,0:T(8,128)(2,1)}) custom-call(bf16[1,128,2048]{2,1,0:T(8,128)(2,1)} %get-tuple-element.170.tokens, bf16[1,128,8192]{2,1,0:T(8,128)(2,1)} %get-tuple-element.171.out_grad, ...), custom_call_target="tpu_custom_call" | custom-call | tf_op jit(solution)/shard_map/cond/branch_10_fun/pallas_call | solution.py:168
  151.0 0.0 copy-done
  151.1 0.0 copy-done.1
  151.1 23.9 %shard_map.102 = (f32[1,2048,1024]{2,1,0:T(8,128)}, bf16[1,2048,1024]{2,1,0:T(8,128)(2,1)}, bf16[1,2048,1024]{2,1,0:T(8,128)(2,1)}, bf16[1,1024,1024]{2,1,0:T(8,128)(2,1)}) custom-call(s32[4]{0:T(128)S(1)} %copy-done, s32[4]{0:T(128)S(1)} %copy-done.1, s32[1]{0:T(128)} %bitcast.place, bf16[1024,2048]{1,0:T(8,128)(2,1)} %get-tuple-element.189.inputs, ...), custom_call_target="tpu_custom_call" | custom-call | tf_op jit(solution)/shard_map/pallas_call | solution.py:244
Async XLA Ops:
  2.6 148.5 %copy-start = (s32[4]{0:T(128)S(1)}, s32[4]{0:T(128)}, u32[]{:S(2)}) copy-start(s32[4]{0:T(128)} %source.1) | copy-start | bytes 52
  2.6 148.5 %copy-start.1 = (s32[4]{0:T(128)S(1)}, s32[4]{0:T(128)}, u32[]{:S(2)}) copy-start(s32[4]{0:T(128)} %perturb.1) | copy-start | bytes 52
where the time goes:
time: 177 us; the launch traced here: 175 us
  Pallas kernels  172 us (97%)
    pallas_call x1, Pallas kernels, exchange(): pl.pallas_call(functools.partial(exchange_kernel, loser, anchor, chunk),...  148 us
    pallas_call x1, Pallas kernels, update(): pl.pallas_call(update_kernel, out_shape=(jax.ShapeDtypeStruct((1, depth,...  23.9 us

commit v1 on v0

--- a/solution.py
+++ b/solution.py
@@ -194,7 +194,7 @@
 
 
 def update_kernel(
-    source, perturb, place, inputs, cols, own_master, own_first, own_second, got_master, got_first, got_second,
+    part_rows, source, perturb, place, inputs, cols, own_master, own_first, own_second, got_master, got_first, got_second,
     new_master, new_first, new_second, gate_out, total,
 ):
     step = pl.program_id(0)
@@ -203,20 +203,25 @@
     rate = jnp.float32(0.0)
     for index, factor in enumerate(rate_factors):
         rate = jnp.where(level == index, np.float32(base_rate) * np.float32(factor), rate)
-    block = inputs[...]
-    grad = lax.dot_general(
-        block, cols[...], (((0,), (0,)), ((), ())), preferred_element_type=jnp.float32
-    )
-    weight = jnp.where(is_taken, got_master[...].astype(jnp.float32), own_master[0])
-    first_old = jnp.where(is_taken, got_first[...], own_first[0]).astype(jnp.float32)
-    second_old = jnp.where(is_taken, got_second[...], own_second[0]).astype(jnp.float32)
-    first = 0.9 * first_old + 0.1 * grad
-    second = 0.95 * second_old + 0.05 * grad * grad
-    updated = weight - rate * (first / (jnp.sqrt(second) + epsilon) + decay * weight)
-    new_master[0] = updated
-    new_first[0] = first.astype(jnp.bfloat16)
-    new_second[0] = second.astype(jnp.bfloat16)
-    part = jnp.dot(block, updated.astype(jnp.bfloat16), preferred_element_type=jnp.float32)
+    block = inputs.shape[1]
+    halves = []
+    for low in range(0, block, part_rows):
+        at = slice(low, low + part_rows)
+        grad = lax.dot_general(
+            inputs[:, at], cols[...], (((0,), (0,)), ((), ())), preferred_element_type=jnp.float32
+        )
+        weight = jnp.where(is_taken, got_master[at].astype(jnp.float32), own_master[0, at])
+        first_old = jnp.where(is_taken, got_first[at], own_first[0, at]).astype(jnp.float32)
+        second_old = jnp.where(is_taken, got_second[at], own_second[0, at]).astype(jnp.float32)
+        first = 0.9 * first_old + 0.1 * grad
+        second = 0.95 * second_old + 0.05 * grad * grad
+        updated = weight - rate * (first / (jnp.sqrt(second) + epsilon) + decay * weight)
+        new_master[0, at] = updated
+        new_first[0, at] = first.astype(jnp.bfloat16)
+        new_second[0, at] = second.astype(jnp.bfloat16)
+        halves.append(updated.astype(jnp.bfloat16))
+    half = jnp.concatenate(halves, axis=0)
+    part = jnp.dot(inputs[...], half, preferred_element_type=jnp.float32)
 
     @pl.when(step == 0)
     def _():
@@ -234,7 +239,7 @@
 def update(source, perturb, place, gathered, cols, master, first, second, got_master, got_first, got_second):
     count, depth = gathered.shape
     width = cols.shape[1]
-    block = 256
+    block, part_rows = 512, 256
 
     own = pl.BlockSpec(
         (1, block, width), lambda i, s, p, m: (0, jnp.where(s[m[0]] == m[0], i, 0), 0)
@@ -242,7 +247,7 @@
     got = pl.BlockSpec((block, width), lambda i, s, p, m: (jnp.where(s[m[0]] == m[0], 0, i), 0))
     new = pl.BlockSpec((1, block, width), lambda i, s, p, m: (0, i, 0))
     return pl.pallas_call(
-        update_kernel,
+        functools.partial(update_kernel, part_rows),
         out_shape=(
             jax.ShapeDtypeStruct((1, depth, width), jnp.float32),
             jax.ShapeDtypeStruct((1, depth, width), jnp.bfloat16),

time: 177 us -> 175 us (0.989)
  Pallas kernels: 172 us -> 169 us
    pallas_call x1, Pallas kernels: 23.9 us -> 21.8 us  [update(): pl.pallas_call(functools.partial(update_kernel, part_rows), out_shape=(ja...]
where the time goes in v1:
time: 175 us; the launch traced here: 172 us
  Pallas kernels  169 us (97%)
    pallas_call x1, Pallas kernels, exchange(): pl.pallas_call(functools.partial(exchange_kernel, loser, anchor, chunk),...  148 us
    pallas_call x1, Pallas kernels, update(): pl.pallas_call(functools.partial(update_kernel, part_rows), out_shape=(ja...  21.8 us

profile of v1, /device:TPU:2, one launch (start us, length us, event | category | flops | bytes accessed | tf_op | source)
XLA Modules:
  0.0 172.4 jit_solution(2511900438147724563)
XLA Ops:
  0.6 1.3 fusion
  2.6 0.0 copy-start
  2.6 0.0 copy-start.1
  2.6 147.8 %conditional.1 = ((bf16[1024,2048]{1,0:T(8,128)(2,1)}, bf16[1024,1024]{1,0:T(8,128)(2,1)S(1)}, bf16[2048,1024]{1,0:T(8,128)(2,1)}, bf16[2048,1024]{1,0:T(8,128)(2,1)}, bf16[2048,1024]{1,0:T(8,128)(2,1)})) conditional(s32[]{:T(128)} %clamp.3, (bf16[1,128,2048]{2,1,0:T(8,128)(2,1)}, bf16[1,128,8192]{2,1,0:T(8,128)(2,1)}, ...), branch_computations={%region_1.2_spmd, %region_2.3_spmd, %region_3.4_spmd, %region_4.5_... | conditional | bytes 8 | solution.py:289
  2.6 147.5 %branch_2_fun.1 = (bf16[1024,2048]{1,0:T(8,128)(2,1)}, bf16[1024,1024]{1,0:T(8,128)(2,1)S(1)}, bf16[2048,1024]{1,0:T(8,128)(2,1)}, bf16[2048,1024]{1,0:T(8,128)(2,1)}, bf16[2048,1024]{1,0:T(8,128)(2,1)}) custom-call(bf16[1,128,2048]{2,1,0:T(8,128)(2,1)} %get-tuple-element.130.tokens, bf16[1,128,8192]{2,1,0:T(8,128)(2,1)} %get-tuple-element.131.out_grad, ...), custom_call_target="tpu_custom_call" | custom-call | tf_op jit(solution)/shard_map/cond/branch_2_fun/pallas_call | solution.py:168
  150.4 0.0 copy-done
  150.4 0.0 copy-done.1
  150.4 21.8 %shard_map.102 = (f32[1,2048,1024]{2,1,0:T(8,128)}, bf16[1,2048,1024]{2,1,0:T(8,128)(2,1)}, bf16[1,2048,1024]{2,1,0:T(8,128)(2,1)}, bf16[1,1024,1024]{2,1,0:T(8,128)(2,1)}) custom-call(s32[4]{0:T(128)S(1)} %copy-done, s32[4]{0:T(128)S(1)} %copy-done.1, s32[1]{0:T(128)} %bitcast.place, bf16[1024,2048]{1,0:T(8,128)(2,1)} %get-tuple-element.189.inputs, ...), custom_call_target="tpu_custom_call" | custom-call | tf_op jit(solution)/shard_map/pallas_call | solution.py:249
Async XLA Ops:
  2.6 147.8 %copy-start = (s32[4]{0:T(128)S(1)}, s32[4]{0:T(128)}, u32[]{:S(2)}) copy-start(s32[4]{0:T(128)} %source.1) | copy-start | bytes 52
  2.6 147.8 %copy-start.1 = (s32[4]{0:T(128)S(1)}, s32[4]{0:T(128)}, u32[]{:S(2)}) copy-start(s32[4]{0:T(128)} %perturb.1) | copy-start | bytes 52
